TPU v7x, 32 devices: a whole 2x2x4 slice. The times are simulated.
32 devices in a mesh: blk: 8 (over z, x), head: 4 (over y, core).
Axes of the slice: x: 2, y: 2, z: 4, core: 2. Of those that a mesh axis runs over, the one named last changes fastest.
Arguments:
- qkv_rows: bfloat16 [8192, 3, 1024], P(('blk', 'head')), may hold values from -10 to 10
- neighbours: int32 [64, 32], P('blk'), may hold values from 0 to 63, as said below
- w_out: bfloat16 [1024, 1024], replicated, may hold values from -0.1875 to 0.1875
Outputs:
- projected: bfloat16 [8192, 1024], P(('blk', 'head'))
Inputs may be any that keep to these rules, and one draw needn't show every extreme that they name: `neighbours`: row b lists 32 different key blocks, the first being b itself; the others lie spread over the whole sequence.
All inputs are finite; a program needn't handle non-finite values.
Results may differ from a plain program's by a relative error of at most 0.0057.
Values may be sent and summed in bfloat16 or wider, within the bound.
A program may use at most 128 MiB of HBM per device.

v0:
```python
import math

import jax
import jax.numpy as jnp
from jax import lax
from jax.sharding import PartitionSpec as P

HD = 64
BLOCK = 128
NBR = 32


def shortened(shard):

    def short(part):
        return part.astype(jnp.bfloat16) if part.dtype == jnp.float32 else part

    return jax.tree.map(short, shard)


def attend_all(queries, pairs, listed):
    head_width = queries.shape[1]
    per_device = head_width // HD
    block_count = listed.shape[0]
    groups = block_count // 4
    query_groups = queries.reshape(groups, 4, BLOCK, head_width)
    key_blocks = pairs.reshape(-1, BLOCK, 2 * head_width)
    list_groups = listed.reshape(groups, 4, NBR)
    scaling = 1.0 / math.sqrt(HD)

    def attend_group(bundle):
        query_group, group_list = bundle
        picked = key_blocks[group_list].reshape(4, NBR * BLOCK, 2 * head_width)
        outputs = []
        for local_head in range(per_device):
            low = local_head * HD
            query_part = query_group[:, :, low : low + HD]
            key_part = picked[:, :, low : low + HD]
            value_part = picked[:, :, head_width + low : head_width + low + HD]
            scores = (
                jnp.einsum("gqd,gkd->gqk", query_part, key_part, preferred_element_type=jnp.float32)
                * scaling
            )
            scores = scores - jnp.max(scores, axis=-1, keepdims=True)
            powers = jnp.exp(scores)
            weights = (powers / jnp.sum(powers, axis=-1, keepdims=True)).astype(jnp.bfloat16)
            outputs.append(
                jnp.einsum("gqk,gkd->gqd", weights, value_part, preferred_element_type=jnp.float32)
            )
        result_rows = jnp.concatenate(outputs, axis=-1)
        return result_rows.astype(jnp.bfloat16)

    attended = lax.map(attend_group, (query_groups, list_groups))
    return attended.reshape(-1, head_width)


def shards(qkv_rows, neighbours, w_out):
    arrived = lax.all_to_all(qkv_rows, "head", split_axis=2, concat_axis=0, tiled=True)
    head_width = arrived.shape[2]
    flat_rows = arrived.reshape(arrived.shape[0], 3 * head_width)
    queries = flat_rows[:, :head_width]
    pairs = lax.all_gather(flat_rows[:, head_width:], "blk", axis=0, tiled=True)
    attended = attend_all(queries, pairs, neighbours)
    token_rows = lax.all_to_all(
        shortened(attended), "head", split_axis=0, concat_axis=1, tiled=True
    ).astype(attended.dtype)
    return jnp.dot(token_rows, w_out, preferred_element_type=jnp.float32).astype(jnp.bfloat16)


def solution(mesh):
    return jax.shard_map(
        shards,
        mesh=mesh,
        in_specs=(P(("blk", "head"), None, None), P("blk", None), P()),
        out_specs=P(("blk", "head"), None),
        check_vma=False,
    )
```

profile of v0, /device:TPU:0, one launch (start us, length us, event | category | flops | bytes accessed | tf_op | source)
XLA Modules:
  0.0 364.4 jit_solution(7627801929538988681)
XLA Ops:
  6.5 4.3 %copy.27 = bf16[256,3,1024]{0,1,2:T(4,128)(2,1)} copy(bf16[256,3,1024]{2,0,1:T(8,128)(2,1)} %param.5) | data formatting | bytes 3145728 | tf_op args[0]
  10.8 29.9 %all_to_all.34 = bf16[256,3,1024]{0,1,2:T(4,128)(2,1)S(1)} all-to-all(bf16[256,3,1024]{0,1,2:T(4,128)(2,1)} %copy.27), channel_id=1, replica_groups=mesh['blk'=8,'head'=4] {'head'}, dimensions={2} | all-to-all | bytes 3145728 | tf_op jit(solution)/shard_map/all_to_all | solution.py:58
  46.2 124.8 %all-gather.2.cloned.1.call-done = bf16[8192,512]{0,1:T(8,128)(2,1)} async-done(((bf16[1024,512]{0,1:T(8,128)(2,1)}), bf16[8192,512]{0,1:T(8,128)(2,1)}) %all-gather.2.cloned.1.call-update) | async-done | bytes 8388624 | tf_op jit(solution)/shard_map/all_gather | solution.py:62
  171.1 11.9 %copy.34 = bf16[8192,512]{1,0:T(8,128)(2,1)} copy(bf16[8192,512]{0,1:T(8,128)(2,1)} %all-gather.2.cloned.1.call-done) | data formatting | bytes 16777216 | tf_op jit(solution)/shard_map/while | solution.py:53
  183.0 160.1 %while.10 = (s32[]{:T(128)}, bf16[2,4,128,256]{3,2,1,0:T(8,128)(2,1)}, bf16[2,4,128,256]{3,2,1,0:T(8,128)(2,1)S(1)}, s32[2,4,32]{2,1,0:T(4,128)S(1)}, bf16[64,128,512]{2,1,0:T(8,128)(2,1)}, /*index=5*/s32[]{:T(128)}) while((s32[]{:T(128)}, bf16[2,4,128,256]{3,2,1,0:T(8,128)(2,1)}, bf16[2,4,128,256]{3,2,1,0:T(8,128)(2,1)S(1)}, ...), condition=%wide.region_9.10_spmd, body=%wide.region_0.9_spmd.sunk | while | flops 3281161728 | bytes 87318088 | solution.py:53
  205.7 11.5 %gather_fusion = bf16[128,128,512]{2,1,0:T(8,128)(2,1)} fusion(bf16[64,128,512]{2,1,0:T(8,128)(2,1)} %get-tuple-element.100, s32[1024]{0:T(1024)S(1)} %pad_clamp_fusion.2), kind=kCustom, calls=%fused_computation.clone.1 | custom fusion | bytes 33554944 | tf_op jit(solution)/shard_map/while/body/eval_jaxpr/gather | solution.py:33
  217.4 4.8 %fusion.244 = f32[4,128]{1,0:T(4,128)S(1)} fusion(bf16[4,4096,512]{2,1,0:T(8,128)(2,1)} %bitcast.44, bf16[4,128,256]{1,2,0:T(8,128)(2,1)S(1)} %bitcast.53), kind=kOutput, calls=%fused_computation.78.clone.1 | convolution fusion | flops 274731008 | bytes 4261888 | tf_op jit(solution)/shard_map/while/body/eval_jaxpr/sub | solution.py:44
  222.2 7.0 %fusion.245 = bf16[1,4,128,64]{2,3,1,0:T(8,128)(2,1)S(1)} fusion(bf16[4,4096,512]{2,1,0:T(8,128)(2,1)} %bitcast.45, f32[4,128]{1,0:T(4,128)S(1)} %fusion.244, bf16[4,128,256]{1,2,0:T(8,128)(2,1)S(1)} %bitcast.54), kind=kOutput, calls=%fused_computation.48.clone.1 | convolution fusion | flops 545296896 | bytes 8521728 | tf_op jit(solution)/shard_map/while/body/eval_jaxpr/gqk,gkd->gqd/dot_general | solution.py:48
  229.3 6.1 %fusion.242 = f32[4,128]{1,0:T(4,128)S(1)} fusion(bf16[4,4096,512]{2,1,0:T(8,128)(2,1)} %bitcast.46, bf16[4,128,256]{1,2,0:T(8,128)(2,1)S(1)} %bitcast.55), kind=kOutput, calls=%fused_computation.77.clone.1 | convolution fusion | flops 274731008 | bytes 4261888 | tf_op jit(solution)/shard_map/while/body/eval_jaxpr/sub | solution.py:44
  235.4 10.0 %fusion.243 = bf16[1,4,128,64]{2,3,1,0:T(8,128)(2,1)S(1)} fusion(bf16[4,4096,512]{2,1,0:T(8,128)(2,1)} %bitcast.47, f32[4,128]{1,0:T(4,128)S(1)} %fusion.242, bf16[4,128,256]{1,2,0:T(8,128)(2,1)S(1)} %bitcast.56), kind=kOutput, calls=%fused_computation.47.clone.1 | convolution fusion | flops 545296896 | bytes 8521728 | tf_op jit(solution)/shard_map/while/body/eval_jaxpr/gqk,gkd->gqd/dot_general | solution.py:48
  245.4 4.8 %fusion.240 = f32[4,128]{1,0:T(4,128)S(1)} fusion(bf16[4,4096,512]{2,1,0:T(8,128)(2,1)} %bitcast.48, bf16[4,128,256]{1,2,0:T(8,128)(2,1)S(1)} %bitcast.57), kind=kOutput, calls=%fused_computation.76.clone.1 | convolution fusion | flops 274731008 | bytes 4261888 | tf_op jit(solution)/shard_map/while/body/eval_jaxpr/sub | solution.py:44
  250.2 7.0 %fusion.241 = bf16[1,4,128,64]{2,3,1,0:T(8,128)(2,1)S(1)} fusion(bf16[4,4096,512]{2,1,0:T(8,128)(2,1)} %bitcast.49, f32[4,128]{1,0:T(4,128)S(1)} %fusion.240, bf16[4,128,256]{1,2,0:T(8,128)(2,1)S(1)} %bitcast.58), kind=kOutput, calls=%fused_computation.46.clone.1 | convolution fusion | flops 545296896 | bytes 8521728 | tf_op jit(solution)/shard_map/while/body/eval_jaxpr/gqk,gkd->gqd/dot_general | solution.py:48
  257.3 6.1 %fusion.238 = f32[4,128]{1,0:T(4,128)S(1)} fusion(bf16[4,4096,512]{2,1,0:T(8,128)(2,1)} %bitcast.50, bf16[4,128,256]{1,2,0:T(8,128)(2,1)S(1)} %bitcast.59), kind=kOutput, calls=%fused_computation.75.clone.1 | convolution fusion | flops 274731008 | bytes 4261888 | tf_op jit(solution)/shard_map/while/body/eval_jaxpr/sub | solution.py:44
  263.4 10.0 %fusion.239 = bf16[1,4,128,64]{2,3,1,0:T(8,128)(2,1)S(1)} fusion(bf16[4,4096,512]{2,1,0:T(8,128)(2,1)} %bitcast.51, f32[4,128]{1,0:T(4,128)S(1)} %fusion.238, bf16[4,128,256]{1,2,0:T(8,128)(2,1)S(1)} %bitcast.60), kind=kOutput, calls=%fused_computation.45.clone.1 | convolution fusion | flops 545296896 | bytes 8521728 | tf_op jit(solution)/shard_map/while/body/eval_jaxpr/gqk,gkd->gqd/dot_general | solution.py:48
  274.5 11.5 %gather_fusion = bf16[128,128,512]{2,1,0:T(8,128)(2,1)} fusion(bf16[64,128,512]{2,1,0:T(8,128)(2,1)} %get-tuple-element.100, s32[1024]{0:T(1024)S(1)} %pad_clamp_fusion.2), kind=kCustom, calls=%fused_computation.clone.1 | custom fusion | bytes 33554944 | tf_op jit(solution)/shard_map/while/body/eval_jaxpr/gather | solution.py:33
  286.2 4.8 %fusion.244 = f32[4,128]{1,0:T(4,128)S(1)} fusion(bf16[4,4096,512]{2,1,0:T(8,128)(2,1)} %bitcast.44, bf16[4,128,256]{1,2,0:T(8,128)(2,1)S(1)} %bitcast.53), kind=kOutput, calls=%fused_computation.78.clone.1 | convolution fusion | flops 274731008 | bytes 4261888 | tf_op jit(solution)/shard_map/while/body/eval_jaxpr/sub | solution.py:44
  291.0 7.0 %fusion.245 = bf16[1,4,128,64]{2,3,1,0:T(8,128)(2,1)S(1)} fusion(bf16[4,4096,512]{2,1,0:T(8,128)(2,1)} %bitcast.45, f32[4,128]{1,0:T(4,128)S(1)} %fusion.244, bf16[4,128,256]{1,2,0:T(8,128)(2,1)S(1)} %bitcast.54), kind=kOutput, calls=%fused_computation.48.clone.1 | convolution fusion | flops 545296896 | bytes 8521728 | tf_op jit(solution)/shard_map/while/body/eval_jaxpr/gqk,gkd->gqd/dot_general | solution.py:48
  298.0 6.1 %fusion.242 = f32[4,128]{1,0:T(4,128)S(1)} fusion(bf16[4,4096,512]{2,1,0:T(8,128)(2,1)} %bitcast.46, bf16[4,128,256]{1,2,0:T(8,128)(2,1)S(1)} %bitcast.55), kind=kOutput, calls=%fused_computation.77.clone.1 | convolution fusion | flops 274731008 | bytes 4261888 | tf_op jit(solution)/shard_map/while/body/eval_jaxpr/sub | solution.py:44
  304.1 10.0 %fusion.243 = bf16[1,4,128,64]{2,3,1,0:T(8,128)(2,1)S(1)} fusion(bf16[4,4096,512]{2,1,0:T(8,128)(2,1)} %bitcast.47, f32[4,128]{1,0:T(4,128)S(1)} %fusion.242, bf16[4,128,256]{1,2,0:T(8,128)(2,1)S(1)} %bitcast.56), kind=kOutput, calls=%fused_computation.47.clone.1 | convolution fusion | flops 545296896 | bytes 8521728 | tf_op jit(solution)/shard_map/while/body/eval_jaxpr/gqk,gkd->gqd/dot_general | solution.py:48
  314.2 4.8 %fusion.240 = f32[4,128]{1,0:T(4,128)S(1)} fusion(bf16[4,4096,512]{2,1,0:T(8,128)(2,1)} %bitcast.48, bf16[4,128,256]{1,2,0:T(8,128)(2,1)S(1)} %bitcast.57), kind=kOutput, calls=%fused_computation.76.clone.1 | convolution fusion | flops 274731008 | bytes 4261888 | tf_op jit(solution)/shard_map/while/body/eval_jaxpr/sub | solution.py:44
  319.0 7.0 %fusion.241 = bf16[1,4,128,64]{2,3,1,0:T(8,128)(2,1)S(1)} fusion(bf16[4,4096,512]{2,1,0:T(8,128)(2,1)} %bitcast.49, f32[4,128]{1,0:T(4,128)S(1)} %fusion.240, bf16[4,128,256]{1,2,0:T(8,128)(2,1)S(1)} %bitcast.58), kind=kOutput, calls=%fused_computation.46.clone.1 | convolution fusion | flops 545296896 | bytes 8521728 | tf_op jit(solution)/shard_map/while/body/eval_jaxpr/gqk,gkd->gqd/dot_general | solution.py:48
  326.1 6.1 %fusion.238 = f32[4,128]{1,0:T(4,128)S(1)} fusion(bf16[4,4096,512]{2,1,0:T(8,128)(2,1)} %bitcast.50, bf16[4,128,256]{1,2,0:T(8,128)(2,1)S(1)} %bitcast.59), kind=kOutput, calls=%fused_computation.75.clone.1 | convolution fusion | flops 274731008 | bytes 4261888 | tf_op jit(solution)/shard_map/while/body/eval_jaxpr/sub | solution.py:44
  332.2 10.0 %fusion.239 = bf16[1,4,128,64]{2,3,1,0:T(8,128)(2,1)S(1)} fusion(bf16[4,4096,512]{2,1,0:T(8,128)(2,1)} %bitcast.51, f32[4,128]{1,0:T(4,128)S(1)} %fusion.238, bf16[4,128,256]{1,2,0:T(8,128)(2,1)S(1)} %bitcast.60), kind=kOutput, calls=%fused_computation.45.clone.1 | convolution fusion | flops 545296896 | bytes 8521728 | tf_op jit(solution)/shard_map/while/body/eval_jaxpr/gqk,gkd->gqd/dot_general | solution.py:48
  343.2 12.3 %all_to_all.35 = bf16[4,256,256]{2,1,0:T(8,128)(2,1)S(1)} all-to-all(bf16[4,256,256]{2,1,0:T(8,128)(2,1)} %bitcast.67), channel_id=1, replica_groups=mesh['blk'=8,'head'=4] {'head'}, dimensions={0} | all-to-all | bytes 1048576 | tf_op jit(solution)/shard_map/all_to_all | solution.py:64
  (32 shorter events, 9.5 us)
Async XLA Ops:
  6.5 349.1 %copy-start = (bf16[1024,1024]{1,0:T(8,128)(2,1)S(1)}, bf16[1024,1024]{1,0:T(8,128)(2,1)}, u32[]{:S(2)}) copy-start(bf16[1024,1024]{1,0:T(8,128)(2,1)} %param.7) | copy-start | bytes 6291460
  6.5 164.6 %all-gather.2.cloned.1.call-start = ((), (), s32[]{:S(2)}) async-start(), calls=%async_computation.2 | async-start | bytes 9437184 | tf_op jit(solution)/shard_map/all_gather | solution.py:62
  42.6 1.2 copy-start.1
  46.2 136.8 %copy-start.2 = (s32[8,32]{1,0:T(8,128)S(1)}, s32[8,32]{1,0:T(8,128)}, u32[]{:S(2)}) copy-start(s32[8,32]{1,0:T(8,128)} %param.6) | copy-start | bytes 3076
Sparse Core Ops, SparseCore 0:
  45.1 125.9 all-gather.1
where the time goes:
time: 368 us; the launch traced here: 364 us
  waiting for transfers between devices  125 us (34%)
  matrix products  114 us (31%)
  local copies, waits for them, and re-layouts  47.2 us (13%)
  blocking collectives  42.2 us (11%)
  loops' own time  22.7 us (6%)
  between operations  13.8 us (4%)
    all_gather x1, waiting for transfers between devices, shards(): pairs = lax.all_gather(flat_rows[:, head_width:], 'blk', axis=0, tiled=True)  125 us
    dot_general x8, matrix products, attend_group(): jnp.einsum('gqk,gkd->gqd', weights, value_part, preferred_element_type=jn...  68.3 us
    sub x8, matrix products, attend_group(): scores = scores - jnp.max(scores, axis=-1, keepdims=True)  43.7 us
    all_to_all x1, blocking collectives, shards(): lax.all_to_all(qkv_rows, 'head', split_axis=2, concat_axis=0, tiled=True)  29.9 us
    gather x2, local copies, waits for them, and re-layouts, attend_group(): picked = key_blocks[group_list].reshape(4, NBR * BLOCK, 2 * head_width)  23 us
    another operation x1, loops' own time, attend_all(): attended = lax.map(attend_group, (query_groups, list_groups))  22.7 us
    all_to_all x1, blocking collectives, shards(): lax.all_to_all(shortened(attended), 'head', split_axis=0, concat_axis=1,...  12.3 us
    while x1, local copies, waits for them, and re-layouts, attend_all(): attended = lax.map(attend_group, (query_groups, list_groups))  11.9 us
  transfers between devices with their start and end apart: 1, of which 1 were waited for; matrix products, arithmetic and copies ran while one was open for 0% of the time, Pallas kernels for 0%

commit v1 on v0

v1 whole, which is shorter than its diff:
```python
import functools
import math

import jax
import jax.numpy as jnp
from jax import lax
from jax.experimental import pallas as pl
from jax.experimental.pallas import tpu as pltpu
from jax.sharding import PartitionSpec as P

HD = 64
BLOCK = 128
CHUNK = 4
MESH = pl.DeviceIdType.MESH
RATE = math.log2(math.e) / math.sqrt(HD)


def xor(a, b, size):
    total, bit = 0, 1
    while bit < size:
        x, y = (a // bit) % 2, (b // bit) % 2
        total = total + (x + y - 2 * x * y) * bit
        bit *= 2
    return total


def kernel(blks, slots, heads, nbr, qkv, near, out, kvp, qp, kv, qs, nbv, nbs, sbuf, mbuf, ob, att,
           kv_s, kv_r, fw_s, fw_r, nb_s, nb_r, q_s, q_r, o_s, o_r, loc):
    share = blks * slots // heads
    tokens = qkv.shape[1]
    per = tokens // BLOCK
    half = tokens // 2
    flat = lax.axis_index("blk") * slots + lax.axis_index("head")
    g, s = flat // share, flat % share

    def device(f):
        return (f // slots, f % slots)

    def peer(i):
        return xor(g, i, heads)

    def remote(src, dst, send, recv, f):
        return pltpu.make_async_remote_copy(
            src_ref=src, dst_ref=dst, send_sem=send, recv_sem=recv,
            device_id=device(f), device_id_type=MESH,
        )

    def kv_copy(i):
        p = peer(i)
        return remote(kvp.at[pl.ds(p * per, per)], kv.at[pl.ds(flat * per, per)], kv_s.at[i], kv_r.at[i],
                      p * share + s)

    def nb_copy(i):
        return remote(near, nbv.at[g], nb_s.at[i], nb_r.at[i], peer(i) * share + s)

    def q_copy(i):
        p = peer(i)
        return remote(qp.at[p], qs.at[g], q_s.at[i], q_r.at[i], p * share + s)

    def o_copy(i):
        p = peer(i)
        return remote(ob.at[p], att.at[g], o_s.at[i], o_r.at[i], p * share + s)

    def forward(i, u):
        slot = pl.ds((peer(i) * share + s) * per, per)
        return remote(kv.at[slot], kv.at[slot], fw_s.at[u - 1, i], fw_r.at[u - 1, i],
                      g * share + (s + u) % share)

    def loop(low, high, body):
        def step(t, carry):
            body(t)
            return carry
        lax.fori_loop(low, high, step, 0)

    barrier = pltpu.get_barrier_semaphore()

    def greet(t):
        pl.semaphore_signal(barrier, inc=1, device_id=device(peer(t) * share + s), device_id_type=MESH)

    loop(1, heads, greet)

    def greet_near(u):
        pl.semaphore_signal(barrier, inc=1, device_id=device(g * share + (s + u) % share), device_id_type=MESH)

    if share > 1:
        loop(1, share, greet_near)

    for h in range(heads):
        cols = slice(h * HD, (h + 1) * HD)
        kvp[h * per:(h + 1) * per] = jnp.concatenate(
            [qkv[1, :, cols], qkv[2, :, cols]], axis=1).reshape(per, BLOCK, 2 * HD)
        qp[h] = jnp.concatenate([qkv[0, :half, cols], qkv[0, half:, cols]], axis=1)
    pl.semaphore_wait(barrier, heads - 1 + share - 1)

    loop(1, heads, lambda t: kv_copy(heads - t).start())
    loop(1, heads, lambda t: nb_copy(heads - t).start())
    loop(1, heads, lambda t: q_copy(heads - t).start())
    own = [
        pltpu.make_async_copy(kvp.at[pl.ds(g * per, per)], kv.at[pl.ds(flat * per, per)], loc.at[0]),
        pltpu.make_async_copy(qp.at[g], qs.at[g], loc.at[1]),
        pltpu.make_async_copy(near, nbv.at[g], loc.at[2]),
    ]
    for copy in own:
        copy.start()
    for copy in own:
        copy.wait()

    def pass_on(i):
        if share > 1:
            loop(1, share, lambda u: forward(i, u).start())

    pass_on(0)

    def arrive(t):
        i = heads - t
        kv_copy(i).wait_recv()
        pass_on(i)

    loop(1, heads, arrive)
    loop(1, heads, lambda t: nb_copy(heads - t).wait_recv())
    table = pltpu.make_async_copy(nbv, nbs, loc.at[3])
    table.start()
    table.wait()
    if share > 1:
        loop(0, heads, lambda i: loop(1, share, lambda u: forward(i, u).wait_recv()))

    hb = per // 2
    chunks = nbr // CHUNK
    wide = CHUNK * BLOCK

    def row_of(p, b):
        return ((p * share + s) % slots) * per + b

    def query(p, b):
        rows = slice((b % hb) * BLOCK, (b % hb + 1) * BLOCK)
        lanes = slice((b // hb) * HD, (b // hb + 1) * HD)
        return jnp.concatenate([qs[p, rows, lanes], jnp.zeros((BLOCK, HD), jnp.bfloat16)], axis=1)

    def keys(p, row, c):
        return jnp.concatenate([kv[nbs[p, row, c * CHUNK + j]] for j in range(CHUNK)], axis=0)

    def scores(q, p, row, c, buf, top):
        part = lax.dot_general(q, keys(p, row, c), (((1,), (1,)), ((), ())), preferred_element_type=jnp.float32)
        sbuf[buf, :, c * wide:(c + 1) * wide] = part
        for j in range(CHUNK):
            piece = part[:, j * BLOCK:(j + 1) * BLOCK]
            top = piece if top is None else jnp.maximum(top, piece)
        return top

    def finish_top(buf, top):
        mbuf[buf] = jnp.broadcast_to(jnp.max(top, axis=1, keepdims=True), (BLOCK, BLOCK))

    def stage(buf, p, b, np_, nb_):
        row, nrow, nbuf = row_of(p, b), row_of(np_, nb_), 1 - buf
        nq = query(np_, nb_)
        top, total, acc = None, None, None
        for c in range(chunks):
            top = scores(nq, np_, nrow, c, nbuf, top)
            m = mbuf[buf]
            pieces = []
            for j in range(CHUNK):
                low = c * wide + j * BLOCK
                e = jnp.exp2((sbuf[buf, :, low:low + BLOCK] - m) * RATE)
                total = e if total is None else total + e
                pieces.append(e.astype(jnp.bfloat16))
            add = jnp.dot(jnp.concatenate(pieces, axis=1), keys(p, row, c), preferred_element_type=jnp.float32)
            acc = add if acc is None else acc + add
        finish_top(nbuf, top)
        return (acc / jnp.sum(total, axis=1, keepdims=True)).astype(jnp.bfloat16)

    top = None
    first = query(g, 0)
    for c in range(chunks):
        top = scores(first, g, row_of(g, 0), c, 0, top)
    finish_top(0, top)

    def source(t):
        i = (heads - t) % heads
        later = jnp.minimum(t + 1, heads - 1)
        ni = (heads - later) % heads
        p, np_ = peer(i), peer(ni)

        @pl.when(t + 1 < heads)
        def _():
            q_copy(ni).wait_recv()

        done = []
        for b in range(per):
            last = b == per - 1
            done.append(stage(b % 2, p, b, np_ if last else p, 0 if last else b + 1))
        for r in range(hb):
            ob[p, r * BLOCK:(r + 1) * BLOCK] = jnp.concatenate([done[r][:, HD:], done[hb + r][:, HD:]], axis=1)

        @pl.when(t > 0)
        def _():
            o_copy(i).start()

    loop(0, heads, source)
    att[g] = ob[g]
    loop(1, heads, lambda t: o_copy(heads - t).wait_recv())
    for k in range(heads // 2):
        even, odd = att[2 * k], att[2 * k + 1]
        cols = slice(2 * k * HD, (2 * k + 2) * HD)
        out[:half, cols] = jnp.concatenate([even[:, :HD], odd[:, :HD]], axis=1)
        out[half:, cols] = jnp.concatenate([even[:, HD:], odd[:, HD:]], axis=1)

    def settle(t):
        i = heads - t
        kv_copy(i).wait_send()
        nb_copy(i).wait_send()
        q_copy(i).wait_send()
        o_copy(i).wait_send()

    loop(1, heads, settle)
    if share > 1:
        loop(0, heads, lambda i: loop(1, share, lambda u: forward(i, u).wait_send()))


def solution(mesh):
    blks, slots = mesh.shape["blk"], mesh.shape["head"]

    def shards(qkv_rows, neighbours, w_out):
        tokens, _, width = qkv_rows.shape
        heads = width // HD
        share = blks * slots // heads
        per = tokens // BLOCK
        nbr = neighbours.shape[1]
        blocks = blks * slots * per
        dma = pltpu.SemaphoreType.DMA
        vmem = pl.BlockSpec(memory_space=pltpu.VMEM)
        attended = pl.pallas_call(
            functools.partial(kernel, blks, slots, heads, nbr),
            out_shape=jax.ShapeDtypeStruct((tokens, width), jnp.bfloat16),
            in_specs=[vmem, vmem],
            out_specs=vmem,
            scratch_shapes=[
                pltpu.VMEM((heads * per, BLOCK, 2 * HD), jnp.bfloat16),
                pltpu.VMEM((heads, tokens // 2, 2 * HD), jnp.bfloat16),
                pltpu.VMEM((blocks, BLOCK, 2 * HD), jnp.bfloat16),
                pltpu.VMEM((heads, tokens // 2, 2 * HD), jnp.bfloat16),
                pltpu.VMEM((heads, *neighbours.shape), jnp.int32),
                pltpu.SMEM((heads, *neighbours.shape), jnp.int32),
                pltpu.VMEM((2, BLOCK, nbr * BLOCK), jnp.float32),
                pltpu.VMEM((2, BLOCK, BLOCK), jnp.float32),
                pltpu.VMEM((heads, tokens // 2, 2 * HD), jnp.bfloat16),
                pltpu.VMEM((heads, tokens // 2, 2 * HD), jnp.bfloat16),
                dma((heads,)), dma((heads,)),
                dma((max(share - 1, 1), heads)), dma((max(share - 1, 1), heads)),
                dma((heads,)), dma((heads,)),
                dma((heads,)), dma((heads,)),
                dma((heads,)), dma((heads,)),
                dma((4,)),
            ],
            compiler_params=pltpu.CompilerParams(
                collective_id=0, has_side_effects=True, vmem_limit_bytes=48 * 2**20
            ),
        )(qkv_rows.transpose(1, 0, 2), neighbours)
        return jnp.dot(attended, w_out, preferred_element_type=jnp.float32).astype(jnp.bfloat16)

    return jax.shard_map(
        shards,
        mesh=mesh,
        in_specs=(P(("blk", "head"), None, None), P("blk", None), P()),
        out_specs=P(("blk", "head"), None),
        check_vma=False,
    )
```

time: 368 us -> 77.7 us (0.21)
  waiting for transfers between devices: 125 us -> 0 us
  matrix products: 114 us -> 1.52 us
  Pallas kernels: 0 us -> 73.7 us
  local copies, waits for them, and re-layouts: 47.2 us -> 2.25 us
  blocking collectives: 42.2 us -> 0 us
  loops' own time: 22.7 us -> 0 us
  between operations: 13.8 us -> 0.02 us
    all_gather x1 -> x0, waiting for transfers between devices: 125 us -> none  [shards(): pairs = lax.all_gather(flat_rows[:, head_width:], 'blk', axis=0, tiled=True)]
    pallas_call x0 -> x1, Pallas kernels: none -> 73.7 us  [shards(): pl.pallas_call(functools.partial(kernel, blks, slots, heads, nbr), out_sh...]
    dot_general x9 -> x1, matrix products: 69.8 us -> 1.52 us  [shards(): jnp.dot(attended, w_out, preferred_element_type=jnp.float32)]
    sub x8 -> x0, matrix products: 43.7 us -> none  [attend_group(): scores = scores - jnp.max(scores, axis=-1, keepdims=True)]
    all_to_all x2 -> x0, blocking collectives: 42.2 us -> none  [the longest x1 29.9 us: shards(): lax.all_to_all(qkv_rows, 'head', split_axis=2, concat_axis=0, tiled=True)]
    gather x2 -> x0, local copies, waits for them, and re-layouts: 23 us -> none  [attend_group(): picked = key_blocks[group_list].reshape(4, NBR * BLOCK, 2 * head_width)]
    another operation x1 -> x0, loops' own time: 22.7 us -> none  [attend_all(): attended = lax.map(attend_group, (query_groups, list_groups))]
    while x1 -> x0, local copies, waits for them, and re-layouts: 11.9 us -> none  [attend_all(): attended = lax.map(attend_group, (query_groups, list_groups))]
  transfers between devices with their start and end apart: 1 -> 0, of which waited for: 1 -> 0; matrix products, arithmetic and copies ran while one was open for 0% -> 0% of each run, Pallas kernels for 0% -> 0%
where the time goes in v1:
time: 77.7 us; the launch traced here: 77.5 us
  Pallas kernels  73.7 us (95%)
  local copies, waits for them, and re-layouts  2.25 us (3%)
  matrix products  1.52 us (2%)
    pallas_call x1, Pallas kernels, shards(): pl.pallas_call(functools.partial(kernel, blks, slots, heads, nbr), out_sh...  73.7 us
    unnamed x6, local copies, waits for them, and re-layouts  2.25 us

profile of v1, /device:TPU:0, one launch (start us, length us, event | category | flops | bytes accessed | tf_op | source)
XLA Modules:
  0.0 77.5 jit_solution(509640601358885979)
XLA Ops:
  0.0 0.0 copy-start
  0.0 0.0 copy-start.1
  0.0 1.6 %copy-done.1 = bf16[256,3,1024]{2,0,1:T(8,128)(2,1)S(1)} copy-done((bf16[256,3,1024]{2,0,1:T(8,128)(2,1)S(1)}, bf16[256,3,1024]{2,0,1:T(8,128)(2,1)}, u32[]{:S(2)}) %copy-start.1) | copy-done | bytes 1572888
  1.6 0.0 copy-start.2
  1.6 0.7 copy-done.2
  2.2 73.7 %shard_map.37 = bf16[256,1024]{1,0:T(8,128)(2,1)S(1)} custom-call(bf16[3,256,1024]{2,1,0:T(8,128)(2,1)S(1)} %bitcast.3, s32[8,32]{1,0:T(8,128)S(1)} %copy-done.2), custom_call_target="tpu_custom_call" | custom-call | tf_op jit(solution)/shard_map/pallas_call | solution.py:231
  76.0 0.0 copy-done
  76.0 1.5 %convolution_convert_fusion = bf16[256,1024]{1,0:T(8,128)(2,1)} fusion(bf16[256,1024]{1,0:T(8,128)(2,1)S(1)} %shard_map.37, bf16[1024,1024]{1,0:T(8,128)(2,1)S(1)} %copy-done), kind=kOutput, calls=%fused_computation | convolution fusion | flops 537133056 | bytes 3145728 | tf_op jit(solution)/shard_map/dot_general | solution.py:258
Async XLA Ops:
  0.0 76.0 %copy-start = (bf16[1024,1024]{1,0:T(8,128)(2,1)S(1)}, bf16[1024,1024]{1,0:T(8,128)(2,1)}, u32[]{:S(2)}) copy-start(bf16[1024,1024]{1,0:T(8,128)(2,1)} %param.5) | copy-start | bytes 6291460
  0.0 1.6 %copy-start.1 = (bf16[256,3,1024]{2,0,1:T(8,128)(2,1)S(1)}, bf16[256,3,1024]{2,0,1:T(8,128)(2,1)}, u32[]{:S(2)}) copy-start(bf16[256,3,1024]{2,0,1:T(8,128)(2,1)} %param.3) | copy-start | bytes 4718596
  1.6 0.7 copy-start.2

commit v2 on v1

v2 whole, which is shorter than its diff:
```python
import functools
import math

import jax
import jax.numpy as jnp
from jax import lax
from jax.experimental import pallas as pl
from jax.experimental.pallas import tpu as pltpu
from jax.sharding import PartitionSpec as P

HD = 64
BLOCK = 128
CHUNK = 8
MESH = pl.DeviceIdType.MESH
RATE = math.log2(math.e) / math.sqrt(HD)


def xor(a, b, size):
    total, bit = 0, 1
    while bit < size:
        x, y = (a // bit) % 2, (b // bit) % 2
        total = total + (x + y - 2 * x * y) * bit
        bit *= 2
    return total


def kernel(blks, slots, heads, nbr, qkv, near, out, kp, vp, qp, kx, vt, qs, nbv, nbs, sbuf, mbuf, ob, att,
           k_s, k_r, v_s, v_r, fk_s, fk_r, fv_s, fv_r, nb_s, nb_r, q_s, q_r, o_s, o_r, loc):
    share = blks * slots // heads
    tokens = qkv.shape[1]
    per = tokens // BLOCK
    half, hb = tokens // 2, per // 2
    flat = lax.axis_index("blk") * slots + lax.axis_index("head")
    g, s = flat // share, flat % share

    def device(f):
        return (f // slots, f % slots)

    def peer(i):
        return xor(g, i, heads)

    def remote(src, dst, send, recv, f):
        return pltpu.make_async_remote_copy(
            src_ref=src, dst_ref=dst, send_sem=send, recv_sem=recv,
            device_id=device(f), device_id_type=MESH,
        )

    def k_copy(i):
        p = peer(i)
        return remote(kp.at[pl.ds(p * hb, hb)], kx.at[pl.ds(flat * per, hb)], k_s.at[i], k_r.at[i], p * share + s)

    def v_copy(i):
        p = peer(i)
        return remote(vp.at[pl.ds(p * per, per)], vt.at[pl.ds(flat * per, per)], v_s.at[i], v_r.at[i], p * share + s)

    def nb_copy(i):
        return remote(near, nbv.at[g], nb_s.at[i], nb_r.at[i], peer(i) * share + s)

    def q_copy(i):
        p = peer(i)
        return remote(qp.at[p], qs.at[g], q_s.at[i], q_r.at[i], p * share + s)

    def o_copy(i):
        p = peer(i)
        return remote(ob.at[p], att.at[g], o_s.at[i], o_r.at[i], p * share + s)

    def k_forward(i, u):
        slot = pl.ds((peer(i) * share + s) * per, hb)
        return remote(kx.at[slot], kx.at[slot], fk_s.at[u - 1, i], fk_r.at[u - 1, i], g * share + (s + u) % share)

    def v_forward(i, u):
        slot = pl.ds((peer(i) * share + s) * per, per)
        return remote(vt.at[slot], vt.at[slot], fv_s.at[u - 1, i], fv_r.at[u - 1, i], g * share + (s + u) % share)

    def loop(low, high, body):
        def step(t, carry):
            body(t)
            return carry
        if high > low:
            lax.fori_loop(low, high, step, 0)

    barrier = pltpu.get_barrier_semaphore()

    def greet(t):
        pl.semaphore_signal(barrier, inc=1, device_id=device(peer(t) * share + s), device_id_type=MESH)

    def greet_near(u):
        pl.semaphore_signal(barrier, inc=1, device_id=device(g * share + (s + u) % share), device_id_type=MESH)

    loop(1, heads, greet)
    loop(1, share, greet_near)

    def halves(part, h):
        cols = slice(h * HD, (h + 1) * HD)
        return jnp.concatenate([qkv[part, :half, cols], qkv[part, half:, cols]], axis=1)

    for h in range(heads):
        kp[h * hb:(h + 1) * hb] = halves(1, h).reshape(hb, BLOCK, 2 * HD)
    pl.semaphore_wait(barrier, heads - 1 + share - 1)
    loop(1, heads, lambda t: k_copy(heads - t).start())
    for b in range(per):
        for k in range(heads // 2):
            flipped = qkv[2, b * BLOCK:(b + 1) * BLOCK, 2 * k * HD:(2 * k + 2) * HD].T
            vp[2 * k * per + b] = flipped[:HD]
            vp[(2 * k + 1) * per + b] = flipped[HD:]
    loop(1, heads, lambda t: v_copy(heads - t).start())
    loop(1, heads, lambda t: nb_copy(heads - t).start())
    for h in range(heads):
        qp[h] = halves(0, h)
    loop(1, heads, lambda t: q_copy(heads - t).start())
    own = [
        pltpu.make_async_copy(kp.at[pl.ds(g * hb, hb)], kx.at[pl.ds(flat * per, hb)], loc.at[0]),
        pltpu.make_async_copy(vp.at[pl.ds(g * per, per)], vt.at[pl.ds(flat * per, per)], loc.at[1]),
        pltpu.make_async_copy(qp.at[g], qs.at[g], loc.at[2]),
        pltpu.make_async_copy(near, nbv.at[g], loc.at[3]),
    ]
    for copy in own:
        copy.start()
    for copy in own:
        copy.wait()

    def turn(f):
        for r in range(hb):
            x = kx[f * per + r]
            kx[f * per + hb + r] = jnp.concatenate([x[:, HD:], x[:, :HD]], axis=1)

    loop(1, share, lambda u: k_forward(0, u).start())
    loop(1, share, lambda u: v_forward(0, u).start())
    turn(flat)

    def k_arrive(t):
        i = heads - t
        k_copy(i).wait_recv()
        loop(1, share, lambda u: k_forward(i, u).start())
        turn(peer(i) * share + s)

    def v_arrive(t):
        i = heads - t
        v_copy(i).wait_recv()
        loop(1, share, lambda u: v_forward(i, u).start())

    def k_passed(t):
        i = (heads - t) % heads

        def from_near(u):
            k_forward(i, u).wait_recv()
            turn(peer(i) * share + (s + share - u) % share)

        loop(1, share, from_near)

    loop(1, heads, k_arrive)
    loop(0, heads, k_passed)
    loop(1, heads, v_arrive)
    loop(1, heads, lambda t: nb_copy(heads - t).wait_recv())
    table = pltpu.make_async_copy(nbv, nbs, loc.at[4])
    table.start()
    table.wait()
    loop(0, heads, lambda i: loop(1, share, lambda u: v_forward(i, u).wait_recv()))

    chunks = nbr // CHUNK
    pairs = CHUNK // 2
    tall = pairs * BLOCK

    def row_of(p, b):
        return ((p * share + s) % slots) * per + b

    def query(p, b):
        rows = slice((b % hb) * BLOCK, (b % hb + 1) * BLOCK)
        q = qs[p, rows, (b // hb) * HD:(b // hb + 1) * HD]
        zero = jnp.zeros((BLOCK, HD), jnp.bfloat16)
        return jnp.concatenate(
            [jnp.concatenate([q, zero], axis=1), jnp.concatenate([zero, q], axis=1)], axis=0)

    def key_pair(n, o):
        turned = (o // per) * per + (o % per + hb) % per
        return jnp.concatenate([kx[n][:, :HD], kx[turned][:, HD:]], axis=1)

    def scores(q, p, row, c, buf, top):
        keys = jnp.concatenate(
            [key_pair(nbs[p, row, c * CHUNK + 2 * j], nbs[p, row, c * CHUNK + 2 * j + 1]) for j in range(pairs)],
            axis=0)
        part = lax.dot_general(keys, q, (((1,), (1,)), ((), ())), preferred_element_type=jnp.float32)
        sbuf[buf, c * tall:(c + 1) * tall] = part
        peak = jnp.max(part.reshape(tall // 8, 8, 2 * BLOCK), axis=0)
        peak = jnp.maximum(peak[:, :BLOCK], peak[:, BLOCK:])
        return peak if top is None else jnp.maximum(top, peak)

    def finish_top(buf, top):
        mbuf[buf] = jnp.broadcast_to(jnp.max(top, axis=0, keepdims=True), (8, BLOCK))

    def stage(buf, p, b, np_, nb_):
        row, nrow, nbuf = row_of(p, b), row_of(np_, nb_), 1 - buf
        nq = query(np_, nb_)
        m = jnp.concatenate([mbuf[buf]] * 2, axis=1)
        top, total, acc = None, None, None
        for c in range(chunks):
            top = scores(nq, np_, nrow, c, nbuf, top)
            e = jnp.exp2((sbuf[buf, c * tall:(c + 1) * tall].reshape(tall // 8, 8, 2 * BLOCK) - m) * RATE)
            add = jnp.sum(e, axis=0)
            total = add if total is None else total + add
            values = jnp.concatenate(
                [jnp.concatenate([vt[nbs[p, row, c * CHUNK + 2 * j + k]] for j in range(pairs)], axis=1)
                 for k in range(2)], axis=0)
            add = jnp.dot(values, e.reshape(tall, 2 * BLOCK).astype(jnp.bfloat16),
                          preferred_element_type=jnp.float32)
            acc = add if acc is None else acc + add
        finish_top(nbuf, top)
        total = jnp.sum(total[:, :BLOCK] + total[:, BLOCK:], axis=0, keepdims=True)
        return ((acc[:HD, :BLOCK] + acc[HD:, BLOCK:]) / total).astype(jnp.bfloat16)

    top = None
    first = query(g, 0)
    for c in range(chunks):
        top = scores(first, g, row_of(g, 0), c, 0, top)
    finish_top(0, top)

    def source(t):
        i = (heads - t) % heads
        later = jnp.minimum(t + 1, heads - 1)
        ni = (heads - later) % heads
        p, np_ = peer(i), peer(ni)

        @pl.when(t + 1 < heads)
        def _():
            q_copy(ni).wait_recv()

        for b in range(per):
            last = b == per - 1
            ob[p, b] = stage(b % 2, p, b, np_ if last else p, 0 if last else b + 1)

        @pl.when(t > 0)
        def _():
            o_copy(i).start()

    loop(0, heads, source)
    att[g] = ob[g]
    loop(1, heads, lambda t: o_copy(heads - t).wait_recv())
    for h in range(heads):
        for b in range(per):
            out[h * HD:(h + 1) * HD, b * BLOCK:(b + 1) * BLOCK] = att[h, b]

    def settle(t):
        i = heads - t
        for copy in (k_copy(i), v_copy(i), nb_copy(i), q_copy(i), o_copy(i)):
            copy.wait_send()

    def settle_near(i):
        def one(u):
            k_forward(i, u).wait_send()
            v_forward(i, u).wait_send()
        loop(1, share, one)

    loop(1, heads, settle)
    loop(0, heads, settle_near)


def solution(mesh):
    blks, slots = mesh.shape["blk"], mesh.shape["head"]

    def shards(qkv_rows, neighbours, w_out):
        tokens, _, width = qkv_rows.shape
        heads = width // HD
        share = blks * slots // heads
        per = tokens // BLOCK
        nbr = neighbours.shape[1]
        blocks = blks * slots * per
        dma = pltpu.SemaphoreType.DMA
        vmem = pl.BlockSpec(memory_space=pltpu.VMEM)
        bf16, f32, i32 = jnp.bfloat16, jnp.float32, jnp.int32
        near = dma((max(share - 1, 1), heads))
        each = dma((heads,))
        attended = pl.pallas_call(
            functools.partial(kernel, blks, slots, heads, nbr),
            out_shape=jax.ShapeDtypeStruct((width, tokens), bf16),
            in_specs=[vmem, vmem],
            out_specs=vmem,
            scratch_shapes=[
                pltpu.VMEM((heads * per // 2, BLOCK, 2 * HD), bf16),
                pltpu.VMEM((heads * per, HD, BLOCK), bf16),
                pltpu.VMEM((heads, tokens // 2, 2 * HD), bf16),
                pltpu.VMEM((blocks, BLOCK, 2 * HD), bf16),
                pltpu.VMEM((blocks, HD, BLOCK), bf16),
                pltpu.VMEM((heads, tokens // 2, 2 * HD), bf16),
                pltpu.VMEM((heads, *neighbours.shape), i32),
                pltpu.SMEM((heads, *neighbours.shape), i32),
                pltpu.VMEM((2, nbr // 2 * BLOCK, 2 * BLOCK), f32),
                pltpu.VMEM((2, 8, BLOCK), f32),
                pltpu.VMEM((heads, per, HD, BLOCK), bf16),
                pltpu.VMEM((heads, per, HD, BLOCK), bf16),
                each, each, each, each, near, near, near, near, each, each, each, each, each, each,
                dma((5,)),
            ],
            compiler_params=pltpu.CompilerParams(
                collective_id=0, has_side_effects=True, vmem_limit_bytes=48 * 2**20
            ),
        )(qkv_rows.transpose(1, 0, 2), neighbours)
        return lax.dot_general(
            attended, w_out, (((0,), (0,)), ((), ())), preferred_element_type=jnp.float32
        ).astype(bf16)

    return jax.shard_map(
        shards,
        mesh=mesh,
        in_specs=(P(("blk", "head"), None, None), P("blk", None), P()),
        out_specs=P(("blk", "head"), None),
        check_vma=False,
    )
```

time: 77.7 us -> 73.9 us (0.951)
  Pallas kernels: 73.7 us -> 69.9 us
    pallas_call x1, Pallas kernels: 73.7 us -> 69.9 us  [shards(): pl.pallas_call(functools.partial(kernel, blks, slots, heads, nbr), out_sh...]
where the time goes in v2:
time: 73.9 us; the launch traced here: 73.7 us
  Pallas kernels  69.9 us (95%)
  local copies, waits for them, and re-layouts  2.25 us (3%)
  matrix products  1.53 us (2%)
    pallas_call x1, Pallas kernels, shards(): pl.pallas_call(functools.partial(kernel, blks, slots, heads, nbr), out_sh...  69.9 us
    unnamed x6, local copies, waits for them, and re-layouts  2.25 us
    dot_general x1, matrix products, shards(): lax.dot_general(attended, w_out, (((0,), (0,)), ((), ())), preferred_elem...  1.53 us

profile of v2, /device:TPU:0, one launch (start us, length us, event | category | flops | bytes accessed | tf_op | source)
XLA Modules:
  0.0 73.7 jit_solution(14534502716014989148)
XLA Ops:
  0.0 0.0 copy-start
  0.0 0.0 copy-start.1
  0.0 1.6 %copy-done.1 = bf16[256,3,1024]{2,0,1:T(8,128)(2,1)S(1)} copy-done((bf16[256,3,1024]{2,0,1:T(8,128)(2,1)S(1)}, bf16[256,3,1024]{2,0,1:T(8,128)(2,1)}, u32[]{:S(2)}) %copy-start.1) | copy-done | bytes 1572888
  1.6 0.0 copy-start.2
  1.6 0.7 copy-done.2
  2.2 69.9 %shard_map.37 = bf16[1024,256]{1,0:T(8,128)(2,1)S(1)} custom-call(bf16[3,256,1024]{2,1,0:T(8,128)(2,1)S(1)} %bitcast.3, s32[8,32]{1,0:T(8,128)S(1)} %copy-done.2), custom_call_target="tpu_custom_call" | custom-call | tf_op jit(solution)/shard_map/pallas_call | solution.py:272
  72.2 0.0 copy-done
  72.2 1.5 %convolution_convert_fusion = bf16[256,1024]{1,0:T(8,128)(2,1)} fusion(bf16[1024,256]{1,0:T(8,128)(2,1)S(1)} %shard_map.37, bf16[1024,1024]{1,0:T(8,128)(2,1)S(1)} %copy-done), kind=kOutput, calls=%fused_computation | convolution fusion | flops 537133056 | bytes 3145728 | tf_op jit(solution)/shard_map/dot_general | solution.py:297
Async XLA Ops:
  0.0 72.2 %copy-start = (bf16[1024,1024]{1,0:T(8,128)(2,1)S(1)}, bf16[1024,1024]{1,0:T(8,128)(2,1)}, u32[]{:S(2)}) copy-start(bf16[1024,1024]{1,0:T(8,128)(2,1)} %param.5) | copy-start | bytes 6291460
  0.0 1.6 %copy-start.1 = (bf16[256,3,1024]{2,0,1:T(8,128)(2,1)S(1)}, bf16[256,3,1024]{2,0,1:T(8,128)(2,1)}, u32[]{:S(2)}) copy-start(bf16[256,3,1024]{2,0,1:T(8,128)(2,1)} %param.3) | copy-start | bytes 4718596
  1.6 0.7 copy-start.2

commit v3 on v2

--- a/solution.py
+++ b/solution.py
@@ -24,10 +24,10 @@
     return total
 
 
-def kernel(blks, slots, heads, nbr, qkv, near, out, kp, vp, qp, kx, vt, qs, nbv, nbs, sbuf, mbuf, ob, att,
+def kernel(blks, slots, heads, nbr, rows, lists, out, qkv, near, kp, vp, qp, kx, vt, qs, nbv, nbs, sbuf, mbuf, ob, att,
            k_s, k_r, v_s, v_r, fk_s, fk_r, fv_s, fv_r, nb_s, nb_r, q_s, q_r, o_s, o_r, loc):
     share = blks * slots // heads
-    tokens = qkv.shape[1]
+    tokens = rows.shape[1]
     per = tokens // BLOCK
     half, hb = tokens // 2, per // 2
     flat = lax.axis_index("blk") * slots + lax.axis_index("head")
@@ -58,7 +58,7 @@
 
     def q_copy(i):
         p = peer(i)
-        return remote(qp.at[p], qs.at[g], q_s.at[i], q_r.at[i], p * share + s)
+        return remote(qp.at[pl.ds(p * per, per)], qs.at[pl.ds(g * per, per)], q_s.at[i], q_r.at[i], p * share + s)
 
     def o_copy(i):
         p = peer(i)
@@ -79,6 +79,11 @@
         if high > low:
             lax.fori_loop(low, high, step, 0)
 
+    loads = [pltpu.make_async_copy(rows.at[k], qkv.at[k], loc.at[5 + k]) for k in range(3)]
+    loads.append(pltpu.make_async_copy(lists, near, loc.at[8]))
+    for k in (1, 2, 3, 0):
+        loads[k].start()
+
     barrier = pltpu.get_barrier_semaphore()
 
     def greet(t):
@@ -90,28 +95,32 @@
     loop(1, heads, greet)
     loop(1, share, greet_near)
 
-    def halves(part, h):
+    loads[1].wait()
+    for h in range(heads):
         cols = slice(h * HD, (h + 1) * HD)
-        return jnp.concatenate([qkv[part, :half, cols], qkv[part, half:, cols]], axis=1)
-
-    for h in range(heads):
-        kp[h * hb:(h + 1) * hb] = halves(1, h).reshape(hb, BLOCK, 2 * HD)
+        kp[h * hb:(h + 1) * hb] = jnp.concatenate(
+            [qkv[1, :half, cols], qkv[1, half:, cols]], axis=1).reshape(hb, BLOCK, 2 * HD)
     pl.semaphore_wait(barrier, heads - 1 + share - 1)
     loop(1, heads, lambda t: k_copy(heads - t).start())
-    for b in range(per):
-        for k in range(heads // 2):
-            flipped = qkv[2, b * BLOCK:(b + 1) * BLOCK, 2 * k * HD:(2 * k + 2) * HD].T
-            vp[2 * k * per + b] = flipped[:HD]
-            vp[(2 * k + 1) * per + b] = flipped[HD:]
+
+    def flip(part, target):
+        loads[part].wait()
+        for b in range(per):
+            for k in range(heads // 2):
+                flipped = qkv[part, b * BLOCK:(b + 1) * BLOCK, 2 * k * HD:(2 * k + 2) * HD].T
+                target[2 * k * per + b] = flipped[:HD]
+                target[(2 * k + 1) * per + b] = flipped[HD:]
+
+    flip(2, vp)
     loop(1, heads, lambda t: v_copy(heads - t).start())
+    loads[3].wait()
     loop(1, heads, lambda t: nb_copy(heads - t).start())
-    for h in range(heads):
-        qp[h] = halves(0, h)
+    flip(0, qp)
     loop(1, heads, lambda t: q_copy(heads - t).start())
     own = [
         pltpu.make_async_copy(kp.at[pl.ds(g * hb, hb)], kx.at[pl.ds(flat * per, hb)], loc.at[0]),
         pltpu.make_async_copy(vp.at[pl.ds(g * per, per)], vt.at[pl.ds(flat * per, per)], loc.at[1]),
-        pltpu.make_async_copy(qp.at[g], qs.at[g], loc.at[2]),
+        pltpu.make_async_copy(qp.at[pl.ds(g * per, per)], qs.at[pl.ds(g * per, per)], loc.at[2]),
         pltpu.make_async_copy(near, nbv.at[g], loc.at[3]),
     ]
     for copy in own:
@@ -165,9 +174,8 @@
         return ((p * share + s) % slots) * per + b
 
     def query(p, b):
-        rows = slice((b % hb) * BLOCK, (b % hb + 1) * BLOCK)
-        q = qs[p, rows, (b // hb) * HD:(b // hb + 1) * HD]
-        zero = jnp.zeros((BLOCK, HD), jnp.bfloat16)
+        q = qs[p * per + b]
+        zero = jnp.zeros((HD, BLOCK), jnp.bfloat16)
         return jnp.concatenate(
             [jnp.concatenate([q, zero], axis=1), jnp.concatenate([zero, q], axis=1)], axis=0)
 
@@ -179,14 +187,14 @@
         keys = jnp.concatenate(
             [key_pair(nbs[p, row, c * CHUNK + 2 * j], nbs[p, row, c * CHUNK + 2 * j + 1]) for j in range(pairs)],
             axis=0)
-        part = lax.dot_general(keys, q, (((1,), (1,)), ((), ())), preferred_element_type=jnp.float32)
+        part = jnp.dot(keys, q, preferred_element_type=jnp.float32)
         sbuf[buf, c * tall:(c + 1) * tall] = part
-        peak = jnp.max(part.reshape(tall // 8, 8, 2 * BLOCK), axis=0)
-        peak = jnp.maximum(peak[:, :BLOCK], peak[:, BLOCK:])
+        peak = jnp.max(part.reshape(tall // 64, 64, 2 * BLOCK), axis=0)
         return peak if top is None else jnp.maximum(top, peak)
 
     def finish_top(buf, top):
-        mbuf[buf] = jnp.broadcast_to(jnp.max(top, axis=0, keepdims=True), (8, BLOCK))
+        top = jnp.max(jnp.maximum(top[:, :BLOCK], top[:, BLOCK:]), axis=0, keepdims=True)
+        mbuf[buf] = jnp.broadcast_to(top, (8, BLOCK))
 
     def stage(buf, p, b, np_, nb_):
         row, nrow, nbuf = row_of(p, b), row_of(np_, nb_), 1 - buf
@@ -196,7 +204,7 @@
         for c in range(chunks):
             top = scores(nq, np_, nrow, c, nbuf, top)
             e = jnp.exp2((sbuf[buf, c * tall:(c + 1) * tall].reshape(tall // 8, 8, 2 * BLOCK) - m) * RATE)
-            add = jnp.sum(e, axis=0)
+            add = jnp.sum(e.reshape(tall // 64, 64, 2 * BLOCK), axis=0)
             total = add if total is None else total + add
             values = jnp.concatenate(
                 [jnp.concatenate([vt[nbs[p, row, c * CHUNK + 2 * j + k]] for j in range(pairs)], axis=1)
@@ -272,15 +280,17 @@
         attended = pl.pallas_call(
             functools.partial(kernel, blks, slots, heads, nbr),
             out_shape=jax.ShapeDtypeStruct((width, tokens), bf16),
-            in_specs=[vmem, vmem],
+            in_specs=[pl.BlockSpec(memory_space=pl.ANY)] * 2,
             out_specs=vmem,
             scratch_shapes=[
+                pltpu.VMEM((3, tokens, width), bf16),
+                pltpu.VMEM(neighbours.shape, i32),
                 pltpu.VMEM((heads * per // 2, BLOCK, 2 * HD), bf16),
                 pltpu.VMEM((heads * per, HD, BLOCK), bf16),
-                pltpu.VMEM((heads, tokens // 2, 2 * HD), bf16),
+                pltpu.VMEM((heads * per, HD, BLOCK), bf16),
                 pltpu.VMEM((blocks, BLOCK, 2 * HD), bf16),
                 pltpu.VMEM((blocks, HD, BLOCK), bf16),
-                pltpu.VMEM((heads, tokens // 2, 2 * HD), bf16),
+                pltpu.VMEM((heads * per, HD, BLOCK), bf16),
                 pltpu.VMEM((heads, *neighbours.shape), i32),
                 pltpu.SMEM((heads, *neighbours.shape), i32),
                 pltpu.VMEM((2, nbr // 2 * BLOCK, 2 * BLOCK), f32),
@@ -288,7 +298,7 @@
                 pltpu.VMEM((heads, per, HD, BLOCK), bf16),
                 pltpu.VMEM((heads, per, HD, BLOCK), bf16),
                 each, each, each, each, near, near, near, near, each, each, each, each, each, each,
-                dma((5,)),
+                dma((9,)),
             ],
             compiler_params=pltpu.CompilerParams(
                 collective_id=0, has_side_effects=True, vmem_limit_bytes=48 * 2**20

time: 73.9 us -> 74.5 us (level)
  no operation moved by 1% of the time
where the time goes in v3:
time: 74.5 us; the launch traced here: 74.3 us
  Pallas kernels  70.5 us (95%)
  local copies, waits for them, and re-layouts  2.25 us (3%)
  matrix products  1.53 us (2%)
    pallas_call x1, Pallas kernels, shards(): pl.pallas_call(functools.partial(kernel, blks, slots, heads, nbr), out_sh...  70.5 us
    unnamed x6, local copies, waits for them, and re-layouts  2.25 us
    dot_general x1, matrix products, shards(): lax.dot_general(attended, w_out, (((0,), (0,)), ((), ())), preferred_elem...  1.53 us

profile of v3, /device:TPU:0, one launch (start us, length us, event | category | flops | bytes accessed | tf_op | source)
XLA Modules:
  0.0 74.3 jit_solution(13846021564889183743)
XLA Ops:
  0.0 0.0 copy-start
  0.0 0.0 copy-start.1
  0.0 1.6 %copy-done.1 = bf16[256,3,1024]{2,0,1:T(8,128)(2,1)S(1)} copy-done((bf16[256,3,1024]{2,0,1:T(8,128)(2,1)S(1)}, bf16[256,3,1024]{2,0,1:T(8,128)(2,1)}, u32[]{:S(2)}) %copy-start.1) | copy-done | bytes 1572888
  1.6 0.0 copy-start.2
  1.6 0.7 copy-done.2
  2.2 70.5 %shard_map.37 = bf16[1024,256]{1,0:T(8,128)(2,1)S(1)} custom-call(bf16[3,256,1024]{2,1,0:T(8,128)(2,1)S(1)} %bitcast.3, s32[8,32]{1,0:T(8,128)S(1)} %copy-done.2), custom_call_target="tpu_custom_call" | custom-call | tf_op jit(solution)/shard_map/pallas_call | solution.py:280
  72.8 0.0 copy-done
  72.8 1.5 %convolution_convert_fusion = bf16[256,1024]{1,0:T(8,128)(2,1)} fusion(bf16[1024,256]{1,0:T(8,128)(2,1)S(1)} %shard_map.37, bf16[1024,1024]{1,0:T(8,128)(2,1)S(1)} %copy-done), kind=kOutput, calls=%fused_computation | convolution fusion | flops 537133056 | bytes 3145728 | tf_op jit(solution)/shard_map/dot_general | solution.py:307
Async XLA Ops:
  0.0 72.8 %copy-start = (bf16[1024,1024]{1,0:T(8,128)(2,1)S(1)}, bf16[1024,1024]{1,0:T(8,128)(2,1)}, u32[]{:S(2)}) copy-start(bf16[1024,1024]{1,0:T(8,128)(2,1)} %param.5) | copy-start | bytes 6291460
  0.0 1.6 %copy-start.1 = (bf16[256,3,1024]{2,0,1:T(8,128)(2,1)S(1)}, bf16[256,3,1024]{2,0,1:T(8,128)(2,1)}, u32[]{:S(2)}) copy-start(bf16[256,3,1024]{2,0,1:T(8,128)(2,1)} %param.3) | copy-start | bytes 4718596
  1.6 0.7 copy-start.2

commit v4 on v3

--- a/solution.py
+++ b/solution.py
@@ -45,6 +45,10 @@
             device_id=device(f), device_id_type=MESH,
         )
 
+    def order(t):
+        u = jnp.maximum(t - 1, 0)
+        return jnp.minimum(t, 1) * (heads - 1 - u // 2 - heads // 2 * (u % 2))
+
     def k_copy(i):
         p = peer(i)
         return remote(kp.at[pl.ds(p * hb, hb)], kx.at[pl.ds(flat * per, hb)], k_s.at[i], k_r.at[i], p * share + s)
@@ -101,7 +105,7 @@
         kp[h * hb:(h + 1) * hb] = jnp.concatenate(
             [qkv[1, :half, cols], qkv[1, half:, cols]], axis=1).reshape(hb, BLOCK, 2 * HD)
     pl.semaphore_wait(barrier, heads - 1 + share - 1)
-    loop(1, heads, lambda t: k_copy(heads - t).start())
+    loop(1, heads, lambda t: k_copy(order(t)).start())
 
     def flip(part, target):
         loads[part].wait()
@@ -112,11 +116,11 @@
                 target[(2 * k + 1) * per + b] = flipped[HD:]
 
     flip(2, vp)
-    loop(1, heads, lambda t: v_copy(heads - t).start())
+    loop(1, heads, lambda t: v_copy(order(t)).start())
     loads[3].wait()
-    loop(1, heads, lambda t: nb_copy(heads - t).start())
+    loop(1, heads, lambda t: nb_copy(order(t)).start())
     flip(0, qp)
-    loop(1, heads, lambda t: q_copy(heads - t).start())
+    loop(1, heads, lambda t: q_copy(order(t)).start())
     own = [
         pltpu.make_async_copy(kp.at[pl.ds(g * hb, hb)], kx.at[pl.ds(flat * per, hb)], loc.at[0]),
         pltpu.make_async_copy(vp.at[pl.ds(g * per, per)], vt.at[pl.ds(flat * per, per)], loc.at[1]),
@@ -138,18 +142,18 @@
     turn(flat)
 
     def k_arrive(t):
-        i = heads - t
+        i = order(t)
         k_copy(i).wait_recv()
         loop(1, share, lambda u: k_forward(i, u).start())
         turn(peer(i) * share + s)
 
     def v_arrive(t):
-        i = heads - t
+        i = order(t)
         v_copy(i).wait_recv()
         loop(1, share, lambda u: v_forward(i, u).start())
 
     def k_passed(t):
-        i = (heads - t) % heads
+        i = order(t)
 
         def from_near(u):
             k_forward(i, u).wait_recv()
@@ -160,7 +164,7 @@
     loop(1, heads, k_arrive)
     loop(0, heads, k_passed)
     loop(1, heads, v_arrive)
-    loop(1, heads, lambda t: nb_copy(heads - t).wait_recv())
+    loop(1, heads, lambda t: nb_copy(order(t)).wait_recv())
     table = pltpu.make_async_copy(nbv, nbs, loc.at[4])
     table.start()
     table.wait()
@@ -223,9 +227,9 @@
     finish_top(0, top)
 
     def source(t):
-        i = (heads - t) % heads
+        i = order(t)
         later = jnp.minimum(t + 1, heads - 1)
-        ni = (heads - later) % heads
+        ni = order(later)
         p, np_ = peer(i), peer(ni)
 
         @pl.when(t + 1 < heads)
@@ -242,13 +246,13 @@
 
     loop(0, heads, source)
     att[g] = ob[g]
-    loop(1, heads, lambda t: o_copy(heads - t).wait_recv())
+    loop(1, heads, lambda t: o_copy(order(t)).wait_recv())
     for h in range(heads):
         for b in range(per):
             out[h * HD:(h + 1) * HD, b * BLOCK:(b + 1) * BLOCK] = att[h, b]
 
     def settle(t):
-        i = heads - t
+        i = order(t)
         for copy in (k_copy(i), v_copy(i), nb_copy(i), q_copy(i), o_copy(i)):
             copy.wait_send()
 
@@ -301,7 +305,7 @@
                 dma((9,)),
             ],
             compiler_params=pltpu.CompilerParams(
-                collective_id=0, has_side_effects=True, vmem_limit_bytes=48 * 2**20
+                collective_id=0, has_side_effects=True, vmem_limit_bytes=62 * 2**20
             ),
         )(qkv_rows.transpose(1, 0, 2), neighbours)
         return lax.dot_general(

time: 74.5 us -> 75.5 us (1.013)
  local copies, waits for them, and re-layouts: 2.25 us -> 0 us
  matrix products: 1.53 us -> 3.3 us
  Pallas kernels: 70.5 us -> 72 us
    unnamed x6 -> x0, local copies, waits for them, and re-layouts: 2.25 us -> none
    dot_general x1, matrix products: 1.53 us -> 3.3 us  [shards(): lax.dot_general(attended, w_out, (((0,), (0,)), ((), ())), preferred_elem...]
    pallas_call x1, Pallas kernels: 70.5 us -> 72 us  [shards(): pl.pallas_call(functools.partial(kernel, blks, slots, heads, nbr), out_sh...]
where the time goes in v4:
time: 75.5 us; the launch traced here: 75.3 us
  Pallas kernels  72 us (95%)
  matrix products  3.3 us (4%)
    pallas_call x1, Pallas kernels, shards(): pl.pallas_call(functools.partial(kernel, blks, slots, heads, nbr), out_sh...  72 us
    dot_general x1, matrix products, shards(): lax.dot_general(attended, w_out, (((0,), (0,)), ((), ())), preferred_elem...  3.3 us

profile of v4, /device:TPU:0, one launch (start us, length us, event | category | flops | bytes accessed | tf_op | source)
XLA Modules:
  0.0 75.3 jit_solution(881464591583029070)
XLA Ops:
  0.0 72.0 %shard_map.37 = bf16[1024,256]{1,0:T(8,128)(2,1)} custom-call(bf16[3,256,1024]{2,1,0:T(8,128)(2,1)} %bitcast.3, s32[8,32]{1,0:T(8,128)} %lists.1), custom_call_target="tpu_custom_call" | custom-call | tf_op jit(solution)/shard_map/pallas_call | solution.py:284
  72.0 3.3 %convolution_convert_fusion = bf16[256,1024]{1,0:T(8,128)(2,1)} fusion(bf16[1024,256]{1,0:T(8,128)(2,1)} %shard_map.37, bf16[1024,1024]{1,0:T(8,128)(2,1)} %param.5), kind=kOutput, calls=%fused_computation | convolution fusion | flops 537133056 | bytes 3145728 | tf_op jit(solution)/shard_map/dot_general | solution.py:311

commit v5 on v4

--- a/solution.py
+++ b/solution.py
@@ -24,7 +24,7 @@
     return total
 
 
-def kernel(blks, slots, heads, nbr, rows, lists, out, qkv, near, kp, vp, qp, kx, vt, qs, nbv, nbs, sbuf, mbuf, ob, att,
+def kernel(blks, slots, heads, nbr, rows, lists, out, qkv, near, kp, vp, qp, kx, vt, qs, nbv, nbs, sbuf, mbuf, pbuf, ob, att,
            k_s, k_r, v_s, v_r, fk_s, fk_r, fv_s, fv_r, nb_s, nb_r, q_s, q_r, o_s, o_r, loc):
     share = blks * slots // heads
     tokens = rows.shape[1]
@@ -66,7 +66,7 @@
 
     def o_copy(i):
         p = peer(i)
-        return remote(ob.at[p], att.at[g], o_s.at[i], o_r.at[i], p * share + s)
+        return remote(ob.at[pl.ds(p * per, per)], att.at[pl.ds(g * per, per)], o_s.at[i], o_r.at[i], p * share + s)
 
     def k_forward(i, u):
         slot = pl.ds((peer(i) * share + s) * per, hb)
@@ -115,12 +115,14 @@
                 target[2 * k * per + b] = flipped[:HD]
                 target[(2 * k + 1) * per + b] = flipped[HD:]
 
-    flip(2, vp)
-    loop(1, heads, lambda t: v_copy(order(t)).start())
+    early = heads // 2
     loads[3].wait()
     loop(1, heads, lambda t: nb_copy(order(t)).start())
     flip(0, qp)
-    loop(1, heads, lambda t: q_copy(order(t)).start())
+    loop(1, early + 1, lambda t: q_copy(order(t)).start())
+    flip(2, vp)
+    loop(1, heads, lambda t: v_copy(order(t)).start())
+    loop(early + 1, heads, lambda t: q_copy(order(t)).start())
     own = [
         pltpu.make_async_copy(kp.at[pl.ds(g * hb, hb)], kx.at[pl.ds(flat * per, hb)], loc.at[0]),
         pltpu.make_async_copy(vp.at[pl.ds(g * per, per)], vt.at[pl.ds(flat * per, per)], loc.at[1]),
@@ -163,13 +165,10 @@
 
     loop(1, heads, k_arrive)
     loop(0, heads, k_passed)
-    loop(1, heads, v_arrive)
     loop(1, heads, lambda t: nb_copy(order(t)).wait_recv())
     table = pltpu.make_async_copy(nbv, nbs, loc.at[4])
     table.start()
     table.wait()
-    loop(0, heads, lambda i: loop(1, share, lambda u: v_forward(i, u).wait_recv()))
-
     chunks = nbr // CHUNK
     pairs = CHUNK // 2
     tall = pairs * BLOCK
@@ -178,10 +177,12 @@
         return ((p * share + s) % slots) * per + b
 
     def query(p, b):
-        q = qs[p * per + b]
+        q = qs[p * per + b].astype(jnp.float32) * RATE
+        high = q.astype(jnp.bfloat16)
+        low = (q - high.astype(jnp.float32)).astype(jnp.bfloat16)
         zero = jnp.zeros((HD, BLOCK), jnp.bfloat16)
         return jnp.concatenate(
-            [jnp.concatenate([q, zero], axis=1), jnp.concatenate([zero, q], axis=1)], axis=0)
+            [jnp.concatenate(x, axis=1) for x in ((high, zero), (zero, high), (low, zero), (zero, low))], axis=0)
 
     def key_pair(n, o):
         turned = (o // per) * per + (o % per + hb) % per
@@ -191,7 +192,7 @@
         keys = jnp.concatenate(
             [key_pair(nbs[p, row, c * CHUNK + 2 * j], nbs[p, row, c * CHUNK + 2 * j + 1]) for j in range(pairs)],
             axis=0)
-        part = jnp.dot(keys, q, preferred_element_type=jnp.float32)
+        part = jnp.dot(jnp.concatenate([keys, keys], axis=1), q, preferred_element_type=jnp.float32)
         sbuf[buf, c * tall:(c + 1) * tall] = part
         peak = jnp.max(part.reshape(tall // 64, 64, 2 * BLOCK), axis=0)
         return peak if top is None else jnp.maximum(top, peak)
@@ -200,25 +201,41 @@
         top = jnp.max(jnp.maximum(top[:, :BLOCK], top[:, BLOCK:]), axis=0, keepdims=True)
         mbuf[buf] = jnp.broadcast_to(top, (8, BLOCK))
 
-    def stage(buf, p, b, np_, nb_):
-        row, nrow, nbuf = row_of(p, b), row_of(np_, nb_), 1 - buf
+    def weights(buf, c):
+        m = jnp.concatenate([mbuf[buf]] * 2, axis=1)
+        e = jnp.exp2(sbuf[buf, c * tall:(c + 1) * tall].reshape(tall // 8, 8, 2 * BLOCK) - m)
+        return e.reshape(tall, 2 * BLOCK).astype(jnp.bfloat16)
+
+    def product(acc, p, row, c, w):
+        ones = jnp.ones((16, tall), jnp.bfloat16)
+        values = jnp.concatenate(
+            [jnp.concatenate([vt[nbs[p, row, c * CHUNK + 2 * j + k]] for j in range(pairs)], axis=1)
+             for k in range(2)] + [ones], axis=0)
+        add = jnp.dot(values, w, preferred_element_type=jnp.float32)
+        return add if acc is None else acc + add
+
+    def divided(acc):
+        total = acc[2 * HD:2 * HD + 1, :BLOCK] + acc[2 * HD:2 * HD + 1, BLOCK:]
+        return ((acc[:HD, :BLOCK] + acc[HD:2 * HD, BLOCK:]) / total).astype(jnp.bfloat16)
+
+    def early_stage(buf, kept, np_, nb_):
+        nrow, nq, top = row_of(np_, nb_), query(np_, nb_), None
+        for c in range(chunks):
+            top = scores(nq, np_, nrow, c, 1 - buf, top)
+            pbuf[kept, c * tall:(c + 1) * tall] = weights(buf, c)
+        finish_top(1 - buf, top)
+
+    def stage(buf, p, b, np_, nb_, op, kept):
+        row, nrow, orow = row_of(p, b), row_of(np_, nb_), row_of(op, b)
         nq = query(np_, nb_)
-        m = jnp.concatenate([mbuf[buf]] * 2, axis=1)
-        top, total, acc = None, None, None
+        top, acc, old = None, None, None
         for c in range(chunks):
-            top = scores(nq, np_, nrow, c, nbuf, top)
-            e = jnp.exp2((sbuf[buf, c * tall:(c + 1) * tall].reshape(tall // 8, 8, 2 * BLOCK) - m) * RATE)
-            add = jnp.sum(e.reshape(tall // 64, 64, 2 * BLOCK), axis=0)
-            total = add if total is None else total + add
-            values = jnp.concatenate(
-                [jnp.concatenate([vt[nbs[p, row, c * CHUNK + 2 * j + k]] for j in range(pairs)], axis=1)
-                 for k in range(2)], axis=0)
-            add = jnp.dot(values, e.reshape(tall, 2 * BLOCK).astype(jnp.bfloat16),
-                          preferred_element_type=jnp.float32)
-            acc = add if acc is None else acc + add
-        finish_top(nbuf, top)
-        total = jnp.sum(total[:, :BLOCK] + total[:, BLOCK:], axis=0, keepdims=True)
-        return ((acc[:HD, :BLOCK] + acc[HD:, BLOCK:]) / total).astype(jnp.bfloat16)
+            top = scores(nq, np_, nrow, c, 1 - buf, top)
+            old = product(old, op, orow, c, pbuf[kept, c * tall:(c + 1) * tall])
+            acc = product(acc, p, row, c, weights(buf, c))
+        finish_top(1 - buf, top)
+        ob[p * per + b] = divided(acc)
+        ob[op * per + b] = divided(old)
 
     top = None
     first = query(g, 0)
@@ -226,30 +243,51 @@
         top = scores(first, g, row_of(g, 0), c, 0, top)
     finish_top(0, top)
 
+    step = -(-(heads - 1) // (early - early // 2))
+
+    def early_source(t):
+        p, np_ = peer(order(t)), peer(order(t + 1))
+        q_copy(order(t + 1)).wait_recv()
+
+        @pl.when(t >= early // 2)
+        def _():
+            low = 1 + (t - early // 2) * step
+
+            def body(k, carry):
+                v_arrive(k)
+                return carry
+            lax.fori_loop(low, jnp.minimum(low + step, heads), body, 0)
+
+        for b in range(per):
+            last = b == per - 1
+            early_stage(b % 2, t * per + b, np_ if last else p, 0 if last else b + 1)
+
     def source(t):
-        i = order(t)
         later = jnp.minimum(t + 1, heads - 1)
-        ni = order(later)
-        p, np_ = peer(i), peer(ni)
+        p, np_, op = peer(order(t)), peer(order(later)), peer(order(t - early))
 
         @pl.when(t + 1 < heads)
         def _():
-            q_copy(ni).wait_recv()
+            q_copy(order(later)).wait_recv()
 
         for b in range(per):
             last = b == per - 1
-            ob[p, b] = stage(b % 2, p, b, np_ if last else p, 0 if last else b + 1)
-
-        @pl.when(t > 0)
+            stage(b % 2, p, b, np_ if last else p, 0 if last else b + 1, op, (t - early) * per + b)
+        o_copy(order(t)).start()
+
+        @pl.when(t > early)
         def _():
-            o_copy(i).start()
-
-    loop(0, heads, source)
-    att[g] = ob[g]
+            o_copy(order(t - early)).start()
+
+    loop(0, early, early_source)
+    loop(0, heads, lambda i: loop(1, share, lambda u: v_forward(i, u).wait_recv()))
+    loop(early, heads, source)
+    for b in range(per):
+        att[g * per + b] = ob[g * per + b]
     loop(1, heads, lambda t: o_copy(order(t)).wait_recv())
     for h in range(heads):
         for b in range(per):
-            out[h * HD:(h + 1) * HD, b * BLOCK:(b + 1) * BLOCK] = att[h, b]
+            out[h * HD:(h + 1) * HD, b * BLOCK:(b + 1) * BLOCK] = att[h * per + b]
 
     def settle(t):
         i = order(t)
@@ -299,8 +337,9 @@
                 pltpu.SMEM((heads, *neighbours.shape), i32),
                 pltpu.VMEM((2, nbr // 2 * BLOCK, 2 * BLOCK), f32),
                 pltpu.VMEM((2, 8, BLOCK), f32),
-                pltpu.VMEM((heads, per, HD, BLOCK), bf16),
-                pltpu.VMEM((heads, per, HD, BLOCK), bf16),
+                pltpu.VMEM((heads // 2 * per, nbr // 2 * BLOCK, 2 * BLOCK), bf16),
+                pltpu.VMEM((heads * per, HD, BLOCK), bf16),
+                pltpu.VMEM((heads * per, HD, BLOCK), bf16),
                 each, each, each, each, near, near, near, near, each, each, each, each, each, each,
                 dma((9,)),
             ],

time: 75.5 us -> 68.9 us (0.913)
  Pallas kernels: 72 us -> 65.5 us
    pallas_call x1, Pallas kernels: 72 us -> 65.5 us  [shards(): pl.pallas_call(functools.partial(kernel, blks, slots, heads, nbr), out_sh...]
where the time goes in v5:
time: 68.9 us; the launch traced here: 68.8 us
  Pallas kernels  65.5 us (95%)
  matrix products  3.29 us (5%)
    pallas_call x1, Pallas kernels, shards(): pl.pallas_call(functools.partial(kernel, blks, slots, heads, nbr), out_sh...  65.5 us
    dot_general x1, matrix products, shards(): lax.dot_general(attended, w_out, (((0,), (0,)), ((), ())), preferred_elem...  3.29 us

profile of v5, /device:TPU:0, one launch (start us, length us, event | category | flops | bytes accessed | tf_op | source)
XLA Modules:
  0.0 68.8 jit_solution(15326506899763672713)
XLA Ops:
  0.0 65.5 %shard_map.37 = bf16[1024,256]{1,0:T(8,128)(2,1)} custom-call(bf16[3,256,1024]{2,1,0:T(8,128)(2,1)} %bitcast.3, s32[8,32]{1,0:T(8,128)} %lists.1), custom_call_target="tpu_custom_call" | custom-call | tf_op jit(solution)/shard_map/pallas_call | solution.py:322
  65.5 3.3 %convolution_convert_fusion = bf16[256,1024]{1,0:T(8,128)(2,1)} fusion(bf16[1024,256]{1,0:T(8,128)(2,1)} %shard_map.37, bf16[1024,1024]{1,0:T(8,128)(2,1)} %param.5), kind=kOutput, calls=%fused_computation | convolution fusion | flops 537133056 | bytes 3145728 | tf_op jit(solution)/shard_map/dot_general | solution.py:350

commit v6 on v5

--- a/solution.py
+++ b/solution.py
@@ -24,7 +24,12 @@
     return total
 
 
-def kernel(blks, slots, heads, nbr, rows, lists, out, qkv, near, kp, vp, qp, kx, vt, qs, nbv, nbs, sbuf, mbuf, pbuf, ob, att,
+def split(heads):
+    late = max(heads // 4, 1)
+    return heads - late, (heads - late) // late
+
+
+def kernel(blks, slots, heads, nbr, rows, lists, weight, out, qkv, near, wbuf, kp, vp, qp, kx, vt, qs, nbv, nbs, sbuf, mbuf, pbuf, ob, att,
            k_s, k_r, v_s, v_r, fk_s, fk_r, fv_s, fv_r, nb_s, nb_r, q_s, q_r, o_s, o_r, loc):
     share = blks * slots // heads
     tokens = rows.shape[1]
@@ -85,7 +90,8 @@
 
     loads = [pltpu.make_async_copy(rows.at[k], qkv.at[k], loc.at[5 + k]) for k in range(3)]
     loads.append(pltpu.make_async_copy(lists, near, loc.at[8]))
-    for k in (1, 2, 3, 0):
+    loads.append(pltpu.make_async_copy(weight, wbuf, loc.at[9]))
+    for k in (1, 3, 0, 2, 4):
         loads[k].start()
 
     barrier = pltpu.get_barrier_semaphore()
@@ -115,7 +121,7 @@
                 target[2 * k * per + b] = flipped[:HD]
                 target[(2 * k + 1) * per + b] = flipped[HD:]
 
-    early = heads // 2
+    early, ratio = split(heads)
     loads[3].wait()
     loop(1, heads, lambda t: nb_copy(order(t)).start())
     flip(0, qp)
@@ -225,17 +231,19 @@
             pbuf[kept, c * tall:(c + 1) * tall] = weights(buf, c)
         finish_top(1 - buf, top)
 
-    def stage(buf, p, b, np_, nb_, op, kept):
-        row, nrow, orow = row_of(p, b), row_of(np_, nb_), row_of(op, b)
+    def stage(buf, p, b, np_, nb_, old):
+        row, nrow = row_of(p, b), row_of(np_, nb_)
         nq = query(np_, nb_)
-        top, acc, old = None, None, None
+        top, acc, kept = None, None, [None] * len(old)
         for c in range(chunks):
             top = scores(nq, np_, nrow, c, 1 - buf, top)
-            old = product(old, op, orow, c, pbuf[kept, c * tall:(c + 1) * tall])
+            for x, (t, op) in enumerate(old):
+                kept[x] = product(kept[x], op, row_of(op, b), c, pbuf[t * per + b, c * tall:(c + 1) * tall])
             acc = product(acc, p, row, c, weights(buf, c))
         finish_top(1 - buf, top)
+        for x, (t, op) in enumerate(old):
+            ob[op * per + b] = divided(kept[x])
         ob[p * per + b] = divided(acc)
-        ob[op * per + b] = divided(old)
 
     top = None
     first = query(g, 0)
@@ -243,28 +251,31 @@
         top = scores(first, g, row_of(g, 0), c, 0, top)
     finish_top(0, top)
 
-    step = -(-(heads - 1) // (early - early // 2))
+    tail = max(early // 4, 1)
+    step = -(-(heads - 1) // tail)
 
     def early_source(t):
         p, np_ = peer(order(t)), peer(order(t + 1))
         q_copy(order(t + 1)).wait_recv()
 
-        @pl.when(t >= early // 2)
+        for b in range(per):
+            last = b == per - 1
+            early_stage(b % 2, t * per + b, np_ if last else p, 0 if last else b + 1)
+
+        @pl.when(t >= early - tail)
         def _():
-            low = 1 + (t - early // 2) * step
+            low = 1 + (t - (early - tail)) * step
 
             def body(k, carry):
                 v_arrive(k)
                 return carry
             lax.fori_loop(low, jnp.minimum(low + step, heads), body, 0)
 
-        for b in range(per):
-            last = b == per - 1
-            early_stage(b % 2, t * per + b, np_ if last else p, 0 if last else b + 1)
-
     def source(t):
         later = jnp.minimum(t + 1, heads - 1)
-        p, np_, op = peer(order(t)), peer(order(later)), peer(order(t - early))
+        p, np_ = peer(order(t)), peer(order(later))
+        first = (t - early) * ratio
+        old = [(first + x, peer(order(first + x))) for x in range(ratio)]
 
         @pl.when(t + 1 < heads)
         def _():
@@ -272,12 +283,12 @@
 
         for b in range(per):
             last = b == per - 1
-            stage(b % 2, p, b, np_ if last else p, 0 if last else b + 1, op, (t - early) * per + b)
+            stage(b % 2, p, b, np_ if last else p, 0 if last else b + 1, old)
+        for x in range(ratio):
+            @pl.when(first + x > 0)
+            def _():
+                o_copy(order(first + x)).start()
         o_copy(order(t)).start()
-
-        @pl.when(t > early)
-        def _():
-            o_copy(order(t - early)).start()
 
     loop(0, early, early_source)
     loop(0, heads, lambda i: loop(1, share, lambda u: v_forward(i, u).wait_recv()))
@@ -285,9 +296,13 @@
     for b in range(per):
         att[g * per + b] = ob[g * per + b]
     loop(1, heads, lambda t: o_copy(order(t)).wait_recv())
-    for h in range(heads):
-        for b in range(per):
-            out[h * HD:(h + 1) * HD, b * BLOCK:(b + 1) * BLOCK] = att[h * per + b]
+    loads[4].wait()
+    flipped = jnp.concatenate(
+        [jnp.concatenate([att[h * per + b] for b in range(per)], axis=1) for h in range(heads)], axis=0).T
+    part = 2 * BLOCK
+    for c in range(wbuf.shape[1] // part):
+        out[:, c * part:(c + 1) * part] = jnp.dot(
+            flipped, wbuf[:, c * part:(c + 1) * part], preferred_element_type=jnp.float32).astype(out.dtype)
 
     def settle(t):
         i = order(t)
@@ -319,14 +334,15 @@
         bf16, f32, i32 = jnp.bfloat16, jnp.float32, jnp.int32
         near = dma((max(share - 1, 1), heads))
         each = dma((heads,))
-        attended = pl.pallas_call(
+        return pl.pallas_call(
             functools.partial(kernel, blks, slots, heads, nbr),
-            out_shape=jax.ShapeDtypeStruct((width, tokens), bf16),
-            in_specs=[pl.BlockSpec(memory_space=pl.ANY)] * 2,
+            out_shape=jax.ShapeDtypeStruct((tokens, w_out.shape[1]), bf16),
+            in_specs=[pl.BlockSpec(memory_space=pl.ANY)] * 3,
             out_specs=vmem,
             scratch_shapes=[
                 pltpu.VMEM((3, tokens, width), bf16),
                 pltpu.VMEM(neighbours.shape, i32),
+                pltpu.VMEM(w_out.shape, bf16),
                 pltpu.VMEM((heads * per // 2, BLOCK, 2 * HD), bf16),
                 pltpu.VMEM((heads * per, HD, BLOCK), bf16),
                 pltpu.VMEM((heads * per, HD, BLOCK), bf16),
@@ -337,19 +353,16 @@
                 pltpu.SMEM((heads, *neighbours.shape), i32),
                 pltpu.VMEM((2, nbr // 2 * BLOCK, 2 * BLOCK), f32),
                 pltpu.VMEM((2, 8, BLOCK), f32),
-                pltpu.VMEM((heads // 2 * per, nbr // 2 * BLOCK, 2 * BLOCK), bf16),
+                pltpu.VMEM((split(heads)[0] * per, nbr // 2 * BLOCK, 2 * BLOCK), bf16),
                 pltpu.VMEM((heads * per, HD, BLOCK), bf16),
                 pltpu.VMEM((heads * per, HD, BLOCK), bf16),
                 each, each, each, each, near, near, near, near, each, each, each, each, each, each,
-                dma((9,)),
+                dma((10,)),
             ],
             compiler_params=pltpu.CompilerParams(
                 collective_id=0, has_side_effects=True, vmem_limit_bytes=62 * 2**20
             ),
-        )(qkv_rows.transpose(1, 0, 2), neighbours)
-        return lax.dot_general(
-            attended, w_out, (((0,), (0,)), ((), ())), preferred_element_type=jnp.float32
-        ).astype(bf16)
+        )(qkv_rows.transpose(1, 0, 2), neighbours, w_out)
 
     return jax.shard_map(
         shards,

time: 68.9 us -> 70.3 us (1.020)
  matrix products: 3.29 us -> 0 us
  Pallas kernels: 65.5 us -> 68.2 us
  local copies, waits for them, and re-layouts: 0 us -> 1.87 us
    dot_general x1 -> x0, matrix products: 3.29 us -> none  [shards(): lax.dot_general(attended, w_out, (((0,), (0,)), ((), ())), preferred_elem...]
    pallas_call x1, Pallas kernels: 65.5 us -> 68.2 us  [shards(): pl.pallas_call(functools.partial(kernel, blks, slots, heads, nbr), out_sh...]
    unnamed x0 -> x1, local copies, waits for them, and re-layouts: none -> 1.87 us
where the time goes in v6:
time: 70.3 us; the launch traced here: 70.1 us
  Pallas kernels  68.2 us (97%)
  local copies, waits for them, and re-layouts  1.87 us (3%)
    pallas_call x1, Pallas kernels, shards(): pl.pallas_call(functools.partial(kernel, blks, slots, heads, nbr), out_sh...  68.2 us
    unnamed x1, local copies, waits for them, and re-layouts  1.87 us

profile of v6, /device:TPU:0, one launch (start us, length us, event | category | flops | bytes accessed | tf_op | source)
XLA Modules:
  0.0 70.1 jit_solution(18054860557580514327)
XLA Ops:
  0.0 68.2 %shard_map.37 = bf16[256,1024]{1,0:T(8,128)(2,1)} custom-call(bf16[3,256,1024]{2,1,0:T(8,128)(2,1)} %bitcast.1, s32[8,32]{1,0:T(8,128)} %lists.1, bf16[1024,1024]{1,0:T(8,128)(2,1)} %weight.1), custom_call_target="tpu_custom_call" | custom-call | tf_op jit(solution)/shard_map/pallas_call | solution.py:337
  68.3 1.9 %copy.5 = bf16[256,1024]{1,0:T(8,128)(2,1)} copy(bf16[256,1024]{1,0:T(8,128)(2,1)} %shard_map.37) | data formatting | bytes 1048576

commit v7 on v5

--- a/solution.py
+++ b/solution.py
@@ -344,7 +344,7 @@
                 dma((9,)),
             ],
             compiler_params=pltpu.CompilerParams(
-                collective_id=0, has_side_effects=True, vmem_limit_bytes=62 * 2**20
+                collective_id=0, has_side_effects=True, vmem_limit_bytes=121 * 2**19
             ),
         )(qkv_rows.transpose(1, 0, 2), neighbours)
         return lax.dot_general(

time: 68.9 us -> 68.5 us (level)
  matrix products: 3.29 us -> 2.56 us
    dot_general x1, matrix products: 3.29 us -> 2.56 us  [shards(): lax.dot_general(attended, w_out, (((0,), (0,)), ((), ())), preferred_elem...]
where the time goes in v7:
time: 68.5 us; the launch traced here: 68.3 us
  Pallas kernels  65.7 us (96%)
  matrix products  2.56 us (4%)
    pallas_call x1, Pallas kernels, shards(): pl.pallas_call(functools.partial(kernel, blks, slots, heads, nbr), out_sh...  65.7 us
    dot_general x1, matrix products, shards(): lax.dot_general(attended, w_out, (((0,), (0,)), ((), ())), preferred_elem...  2.56 us

profile of v7, /device:TPU:0, one launch (start us, length us, event | category | flops | bytes accessed | tf_op | source)
XLA Modules:
  0.0 68.3 jit_solution(2331932377424818145)
XLA Ops:
  0.0 0.0 copy-start
  0.0 65.7 %shard_map.37 = bf16[1024,256]{1,0:T(8,128)(2,1)} custom-call(bf16[3,256,1024]{2,1,0:T(8,128)(2,1)} %bitcast.3, s32[8,32]{1,0:T(8,128)} %lists.1), custom_call_target="tpu_custom_call" | custom-call | tf_op jit(solution)/shard_map/pallas_call | solution.py:322
  65.7 0.0 copy-done
  65.7 2.6 %convolution_convert_fusion = bf16[256,1024]{1,0:T(8,128)(2,1)} fusion(bf16[1024,256]{1,0:T(8,128)(2,1)} %shard_map.37, bf16[1024,1024]{1,0:T(8,128)(2,1)S(1)} %copy-done), kind=kOutput, calls=%fused_computation | convolution fusion | flops 537133056 | bytes 3145728 | tf_op jit(solution)/shard_map/dot_general | solution.py:350
Async XLA Ops:
  0.0 65.7 %copy-start = (bf16[1024,1024]{1,0:T(8,128)(2,1)S(1)}, bf16[1024,1024]{1,0:T(8,128)(2,1)}, u32[]{:S(2)}) copy-start(bf16[1024,1024]{1,0:T(8,128)(2,1)} %param.5) | copy-start | bytes 6291460
